TPU v7x, 32 devices: a whole 2x2x4 slice. The times are simulated.
32 devices in a mesh: space: 16 (over z, y, core), bead: 2 (over x).
Axes of the slice: x: 2, y: 2, z: 4, core: 2. Of those that a mesh axis runs over, the one named last changes fastest.
Arguments:
- positions: float32 [8, 3, 2048], P('bead', None, 'space'), may hold values from 0 to 2
- momenta: float32 [8, 3, 2048], P('bead', None, 'space'), may hold values from -6 to 6
- masses: float32 [2048], P('space'), may hold values from 1 to 4
- features: bfloat16 [8, 2048, 128], P('bead', 'space'), may hold values from -6 to 6
- neighbours: int32 [64, 2048], P(None, 'space'), may hold values from 0 to 383
- images: int32 [64, 2048], P(None, 'space'), may hold values from 0 to 26
- face_map: int32 [2, 16, 128], P(None, 'space'), may hold values from 0 to 127, each once within a row
- w_query: bfloat16 [128, 128], replicated, may hold values from -0.5 to 0.5
- w_key: bfloat16 [128, 128], replicated, may hold values from -0.375 to 0.375
- w_value: bfloat16 [128, 128], replicated, may hold values from -2 to 2
- w_probe: bfloat16 [128, 128], replicated, may hold values from -0.5 to 0.5
- radial_rate: float32 [8], replicated, may hold values from 0.02 to 0.5
Outputs:
- new_positions: float32 [8, 3, 2048], P('bead', None, 'space')
- new_momenta: float32 [8, 3, 2048], P('bead', None, 'space')
Inputs may be any that keep to these rules, and one draw needn't show every extreme that they name: `neighbours`: each entry is a row of the atom's slab's extended table: own atoms first, then the ghosts from the lower slab, then those from the upper slab. `face_map`: each row of a slab's block lists every atom of that slab once.
All inputs are finite; a program needn't handle non-finite values.
Results may differ from a plain program's by a relative error of at most 0.0025.
Values may be sent and summed in bfloat16 or wider, within the bound.
A program may use at most 64 MiB of HBM per device.

v0:
```python
import jax
import jax.numpy as jnp
from jax import lax
from jax.sharding import PartitionSpec as P

STIFFNESS = 1.3
BOX_LENGTH = 2.0
SCORE_CAP = 30.0


def padded(block, sides, width):
    for axis, dim in sides:
        count = lax.axis_size(axis)
        forward = [(i, i + 1) for i in range(count - 1)]
        forward.append((count - 1, 0))
        backward = [(target, source) for source, target in forward]
        low = lax.ppermute(
            lax.slice_in_dim(block, block.shape[dim] - width, None, axis=dim), axis, forward
        )
        high = lax.ppermute(lax.slice_in_dim(block, 0, width, axis=dim), axis, backward)
        block = jnp.concatenate([low, block, high], axis=dim)
    return block


def mode_table(bead_count):
    bead_column = jnp.arange(bead_count).astype(jnp.float32)[:, None]
    mode_row = jnp.arange(bead_count).astype(jnp.float32)[None, :]
    mode_index = jnp.arange(bead_count)[None, :] + jnp.zeros((bead_count, 1), jnp.int32)
    angles = 2.0 * jnp.pi * bead_column * mode_row / bead_count
    wave_norm = jnp.sqrt(jnp.float32(2.0 / bead_count))
    flat_norm = jnp.sqrt(jnp.float32(1.0 / bead_count))
    half_count = bead_count // 2
    entries = jnp.where(
        mode_index < half_count, wave_norm * jnp.cos(angles), wave_norm * jnp.sin(angles)
    )
    entries = jnp.where(mode_index == half_count, flat_norm * jnp.cos(angles), entries)
    entries = jnp.where(mode_index == 0, flat_norm + 0.0 * angles, entries)
    return entries


def frequencies(bead_count):
    mode_float = jnp.arange(bead_count).astype(jnp.float32)
    return 2.0 * STIFFNESS * jnp.sin(jnp.pi * mode_float / bead_count)


def propagate(mode_pos, mode_mom, masses, frequency):
    phase_turn = frequency[:, None, None]
    cosine_turn = jnp.cos(phase_turn)
    sine_turn = jnp.sin(phase_turn)
    safe_turn = jnp.where(phase_turn > 0, phase_turn, 1.0)
    drift_gain = jnp.where(phase_turn > 0, sine_turn / safe_turn, 1.0)
    mass_row = masses[None, None, :]
    next_pos = cosine_turn * mode_pos + drift_gain * mode_mom / mass_row
    next_mom = cosine_turn * mode_mom - mass_row * phase_turn * sine_turn * mode_pos
    return (next_pos, next_mom)


def image_offsets(images):
    offset_x = images % 3 - 1
    offset_y = images // 3 % 3 - 1
    offset_z = images // 9 - 1
    return BOX_LENGTH * jnp.stack([offset_x, offset_y, offset_z]).astype(jnp.float32)


def probe_matrices(own_features, w_query, w_key, w_value, w_probe, head_count):
    atom_count, channels = own_features.shape
    head_size = channels // head_count
    queries = jnp.dot(own_features, w_query, preferred_element_type=jnp.float32).reshape(
        atom_count, head_count, head_size
    )
    probes = jnp.dot(own_features, w_probe, preferred_element_type=jnp.float32).reshape(
        atom_count, head_count, head_size
    )
    key_heads = w_key.astype(jnp.float32).reshape(channels, head_count, head_size)
    value_heads = w_value.astype(jnp.float32).reshape(channels, head_count, head_size)
    key_probe = jnp.einsum("ahd,chd->ahc", queries, key_heads, precision=lax.Precision.HIGHEST)
    value_probe = jnp.einsum("ahd,chd->ahc", probes, value_heads, precision=lax.Precision.HIGHEST)
    return jnp.concatenate([key_probe, value_probe], axis=1).astype(jnp.bfloat16)


def attend_forces(pair_terms, offsets, radial_rate, head_size):
    head_count = radial_rate.shape[0]
    scores = pair_terms[:head_count] * head_size ** (-0.5)
    capped = SCORE_CAP * jnp.tanh(scores / SCORE_CAP)
    distance = jnp.sum(offsets * offsets, axis=0)
    logits = capped - radial_rate[:, None, None] * distance[None]
    weights = jnp.exp(logits)
    attention = weights / jnp.sum(weights, axis=1, keepdims=True)
    coupling = jnp.sum(attention * pair_terms[head_count:], axis=0) * (
        1.0 / (head_count * head_size**0.5)
    )
    return jnp.sum(coupling[None] * offsets, axis=1)


def split_pieces(coordinate_table):
    high_part = coordinate_table.astype(jnp.bfloat16)
    first_rest = coordinate_table - high_part.astype(jnp.float32)
    middle_part = first_rest.astype(jnp.bfloat16)
    low_part = (first_rest - middle_part.astype(jnp.float32)).astype(jnp.bfloat16)
    return jnp.concatenate([high_part, middle_part, low_part], axis=0)


def bead_forces(
    feature_table,
    coordinate_table,
    neighbours,
    images,
    w_query,
    w_key,
    w_value,
    w_probe,
    radial_rate,
):
    near_count, atom_count = neighbours.shape
    table_rows, channels = feature_table.shape
    head_count = radial_rate.shape[0]
    head_size = channels // head_count
    probe_mats = probe_matrices(
        feature_table[:atom_count], w_query, w_key, w_value, w_probe, head_count
    )
    coordinate_pieces = split_pieces(coordinate_table)
    own_coords = coordinate_table[:, :atom_count]
    shift_table = image_offsets(images)
    block_size = min(atom_count, 128)
    block_count = atom_count // block_size
    table_index = jnp.arange(table_rows, dtype=jnp.int32)

    def one_block(block_id):
        selector = (
            neighbours.reshape(near_count * block_size)[:, None] == table_index[None, :]
        ).astype(jnp.bfloat16)
        picked = jnp.dot(selector, feature_table, preferred_element_type=jnp.float32).astype(
            jnp.bfloat16
        )
        gathered = picked.reshape(near_count, block_size, channels)
        picked_pieces = jnp.einsum(
            "pr,mr->pm", coordinate_pieces, selector, preferred_element_type=jnp.float32
        )
        picked_pieces = picked_pieces.reshape(3, 3, near_count, block_size)
        near_coords = picked_pieces[0] + picked_pieces[1] + picked_pieces[2]
        block_offsets = near_coords - own_coords[:, None, :] + shift_table
        pair_terms = jnp.einsum(
            "kac,aec->eka", gathered, probe_mats, preferred_element_type=jnp.float32
        )
        return attend_forces(pair_terms, block_offsets, radial_rate, head_size)

    blocks = lax.map(one_block, jnp.arange(block_count))
    return blocks.transpose(1, 0, 2).reshape(3, atom_count)


def body(
    positions,
    momenta,
    masses,
    features,
    neighbours,
    images,
    face_map,
    w_query,
    w_key,
    w_value,
    w_probe,
    radial_rate,
):
    bead_local = positions.shape[0]
    atom_count = masses.shape[0]
    send_rows = jnp.concatenate([face_map[0, 0], face_map[1, 0]])
    atom_index = jnp.arange(atom_count, dtype=jnp.int32)
    row_select = send_rows[:, None] == atom_index[None, :]
    feature_buffer = jnp.einsum(
        "ra,bac->brc", row_select.astype(jnp.bfloat16), features, preferred_element_type=jnp.float32
    ).astype(jnp.bfloat16)
    coordinate_buffer = jnp.einsum(
        "bca,ra->bcr", positions, row_select.astype(jnp.float32), precision=lax.Precision.HIGHEST
    )
    force_list = []
    feature_halo = padded(feature_buffer, (("space", 1),), atom_count)
    coordinate_halo = padded(coordinate_buffer, (("space", 2),), atom_count)
    for bead_slot in range(bead_local):
        feature_table = jnp.concatenate(
            [
                features[bead_slot],
                feature_halo[bead_slot, :atom_count],
                feature_halo[bead_slot, 3 * atom_count :],
            ],
            axis=0,
        )
        coordinate_table = jnp.concatenate(
            [
                positions[bead_slot],
                coordinate_halo[bead_slot, :, :atom_count],
                coordinate_halo[bead_slot, :, 3 * atom_count :],
            ],
            axis=1,
        )
        force_list.append(
            bead_forces(
                feature_table,
                coordinate_table,
                neighbours,
                images,
                w_query,
                w_key,
                w_value,
                w_probe,
                radial_rate,
            )
        )
    kicked = momenta + jnp.stack(force_list)
    bead_groups = lax.axis_size("bead")
    bead_count = bead_local * bead_groups
    transform = mode_table(bead_count)
    frequency = frequencies(bead_count)
    stacked = jnp.stack([positions, kicked])
    group_id = lax.axis_index("bead")
    own_columns = lax.dynamic_slice_in_dim(transform, group_id * bead_local, bead_local, 1)
    own_frequency = lax.dynamic_slice_in_dim(frequency, group_id * bead_local, bead_local)
    own_bead_rows = lax.dynamic_slice_in_dim(transform, group_id * bead_local, bead_local, 0)
    coeffs = own_columns
    mode_parts = jnp.einsum(
        "bk,sbcn->skcn",
        coeffs,
        lax.all_gather(stacked, "bead", axis=1, tiled=True),
        precision=lax.Precision.HIGHEST,
    )
    next_pos, next_mom = propagate(mode_parts[0], mode_parts[1], masses, own_frequency)
    coeffs = own_bead_rows
    result = jnp.einsum(
        "bk,skcn->sbcn",
        coeffs,
        lax.all_gather(jnp.stack([next_pos, next_mom]), "bead", axis=1, tiled=True),
        precision=lax.Precision.HIGHEST,
    )
    return (result[0], result[1])


def solution(mesh):
    placed = (
        P("bead", None, "space"),
        P("bead", None, "space"),
        P("space"),
        P("bead", "space", None),
        P(None, "space"),
        P(None, "space"),
        P(None, "space", None),
        P(),
        P(),
        P(),
        P(),
        P(),
    )
    return jax.shard_map(
        body,
        mesh=mesh,
        in_specs=placed,
        out_specs=(P("bead", None, "space"), P("bead", None, "space")),
        check_vma=False,
    )
```

profile of v0, /device:TPU:0, one launch (start us, length us, event | category | flops | bytes accessed | tf_op | source)
XLA Modules:
  0.0 88.4 jit_solution(531310310074506892)
XLA Ops:
  0.7 0.7 slice_bitcast_fusion.19
  1.4 0.9 %convolution_bitcast_fusion.2 = f32[4,3,256]{2,0,1:T(4,128)S(1)} fusion(f32[4,3,128]{2,0,1:T(4,128)} %param.12, s32[256]{0:T(256)S(1)} %pad_add_fusion), kind=kOutput, calls=%fused_computation.65 | convolution fusion | flops 4751360 | bytes 19456 | tf_op jit(solution)/shard_map/bca,ra->bcr/dot_general | solution.py:173
  3.0 5.4 %collective-permute-start.3 = (f32[4,3,128]{2,0,1:T(4,128)}, f32[4,3,128]{2,0,1:T(4,128)}, u32[]{:S(2)}, u32[]{:S(2)}) collective-permute-start(f32[4,3,128]{2,0,1:T(4,128)} %get-tuple-element.149), channel_id=1, source_target_pairs={{2,0},{4,2},{6,4},{8,6},{10,8},{12,10},{14,12},{16,14},{18,16},{20... | collective-permute-start | bytes 18440 | tf_op jit(solution)/shard_map/ppermute | solution.py:20
  9.0 1.2 %fusion.52 = bf16[4,256,128]{2,1,0:T(8,128)(2,1)S(1)} fusion(bf16[4,128,128]{2,1,0:T(8,128)(2,1)} %param.15, s32[256]{0:T(256)S(1)} %pad_add_fusion), kind=kOutput, calls=%fused_computation.54 | convolution fusion | flops 33718272 | bytes 394240 | tf_op jit(solution)/shard_map/ra,bac->brc/dot_general | solution.py:170
  10.9 4.4 %collective-permute-start.1 = (bf16[4,128,128]{2,1,0:T(8,128)(2,1)}, bf16[4,128,128]{2,1,0:T(8,128)(2,1)}, u32[]{:S(2)}, u32[]{:S(2)}) collective-permute-start(bf16[4,128,128]{2,1,0:T(8,128)(2,1)} %get-tuple-element.106), channel_id=1, source_target_pairs={{2,0},{4,2},{6,4},{8,6},{10,8},{12,10},{14,12},{16,14},{18,16},{20... | collective-permute-start | bytes 393224 | tf_op jit(solution)/shard_map/ppermute | solution.py:20
  15.3 0.8 fusion.257
  16.2 1.5 %slice_bitcast_fusion.9 = (bf16[128,128]{1,0:T(8,128)(2,1)}, bf16[128,128]{1,0:T(8,128)(2,1)}, bf16[128,128]{1,0:T(8,128)(2,1)}, bf16[128,128]{1,0:T(8,128)(2,1)}) fusion(bf16[4,128,128]{2,1,0:T(8,128)(2,1)} %param.15), kind=kLoop, calls=%fused_computation.227 | loop fusion | bytes 262144 | tf_op jit(solution)/shard_map/squeeze | solution.py:182
  17.7 0.9 copy.152
  18.5 0.9 %fusion.172 = f32[128,8,16]{0,2,1:T(8,128)S(1)} fusion(bf16[8,16,128]{2,1,0:T(8,128)(2,1)S(1)} %bitcast.261, bf16[4,128,128]{2,1,0:T(8,128)(2,1)} %param.15), kind=kOutput, calls=%fused_computation.214 | convolution fusion | flops 4194304 | bytes 131072 | tf_op jit(solution)/shard_map/dot_general | solution.py:71
  19.4 0.9 %fusion.168 = f32[128,8,16]{0,2,1:T(8,128)S(1)} fusion(bf16[8,16,128]{2,1,0:T(8,128)(2,1)S(1)} %bitcast.262, bf16[4,128,128]{2,1,0:T(8,128)(2,1)} %param.15), kind=kOutput, calls=%fused_computation.210 | convolution fusion | flops 4194304 | bytes 131072 | tf_op jit(solution)/shard_map/dot_general | solution.py:71
  20.4 0.9 %copy.150 = bf16[128,128]{0,1:T(8,128)(2,1)S(1)} copy(bf16[128,128]{1,0:T(8,128)(2,1)} %param.19) | data formatting | bytes 65536 | tf_op args[7]
  21.2 0.9 %fusion.174 = f32[128,8,16]{0,2,1:T(8,128)S(1)} fusion(bf16[8,16,128]{2,1,0:T(8,128)(2,1)S(1)} %bitcast.265, bf16[4,128,128]{2,1,0:T(8,128)(2,1)} %param.15), kind=kOutput, calls=%fused_computation.216 | convolution fusion | flops 4194304 | bytes 131072 | tf_op jit(solution)/shard_map/dot_general | solution.py:68
  22.1 0.9 %fusion.170 = f32[128,8,16]{0,2,1:T(8,128)S(1)} fusion(bf16[8,16,128]{2,1,0:T(8,128)(2,1)S(1)} %bitcast.266, bf16[4,128,128]{2,1,0:T(8,128)(2,1)} %param.15), kind=kOutput, calls=%fused_computation.212 | convolution fusion | flops 4194304 | bytes 131072 | tf_op jit(solution)/shard_map/dot_general | solution.py:68
  23.1 0.9 %fusion.164 = f32[128,8,16]{0,2,1:T(8,128)S(1)} fusion(bf16[8,16,128]{2,1,0:T(8,128)(2,1)S(1)} %bitcast.263, bf16[4,128,128]{2,1,0:T(8,128)(2,1)} %param.15), kind=kOutput, calls=%fused_computation.206 | convolution fusion | flops 4194304 | bytes 131072 | tf_op jit(solution)/shard_map/dot_general | solution.py:71
  35.3 1.4 %fusion.213 = f32[8,8]{0,1:T(8,128)} fusion(f32[8]{0:T(128)} %iota_convert_fusion, f32[8]{0:T(128)} %broadcast_multiply_fusion.4, pred[8]{0:T(512)(128)(4,1)} %get-tuple-element.190, pred[8]{0:T(512)(128)(4,1)} %get-tuple-element.191, pred[8]{0:T(512)(128)(4,1)} %iota_compare_fusion.20), kind=kLoop, calls=%fused_computation.287 | loop fusion | flops 640 | bytes 344 | tf_op jit(solution)/shard_map/jit(_where)/select_n | solution.py:37
  36.7 0.8 fusion.256
  40.7 2.3 %fusion.10 = f32[9,8192]{1,0:T(8,128)S(1)} fusion(s32[8192]{0:T(1024)S(1)} %bitcast.296, bf16[3,384]{1,0:T(4,128)(2,1)S(1)} %get-tuple-element.175, bf16[3,384]{1,0:T(4,128)(2,1)S(1)} %get-tuple-element.174, bf16[3,384]{1,0:T(4,128)(2,1)S(1)} %fusion.247), kind=kOutput, calls=%fused_computation.11 | convolution fusion | flops 59789568 | bytes 334592 | tf_op jit(solution)/shard_map/while/body/eval_jaxpr/pr,mr->pm/dot_general | solution.py:136
  43.0 2.3 %fusion.8 = f32[9,8192]{1,0:T(8,128)S(1)} fusion(s32[8192]{0:T(1024)S(1)} %bitcast.297, bf16[3,384]{1,0:T(4,128)(2,1)S(1)} %get-tuple-element.165, bf16[3,384]{1,0:T(4,128)(2,1)S(1)} %get-tuple-element.164, bf16[3,384]{1,0:T(4,128)(2,1)S(1)} %fusion.246), kind=kOutput, calls=%fused_computation.9 | convolution fusion | flops 59789568 | bytes 334592 | tf_op jit(solution)/shard_map/while/body/eval_jaxpr/pr,mr->pm/dot_general | solution.py:136
  47.2 3.2 %fusion.6 = f32[9,8192]{1,0:T(8,128)S(1)} fusion(s32[8192]{0:T(1024)} %bitcast.294, bf16[3,384]{1,0:T(4,128)(2,1)} %get-tuple-element.177, bf16[3,384]{1,0:T(4,128)(2,1)} %get-tuple-element.176, bf16[3,384]{1,0:T(4,128)(2,1)} %fusion.245), kind=kOutput, calls=%fused_computation.7 | convolution fusion | flops 59789568 | bytes 334592 | tf_op jit(solution)/shard_map/while/body/eval_jaxpr/pr,mr->pm/dot_general | solution.py:136
  50.5 2.3 %fusion.4 = f32[9,8192]{1,0:T(8,128)S(1)} fusion(s32[8192]{0:T(1024)S(1)} %bitcast.298, bf16[3,384]{1,0:T(4,128)(2,1)S(1)} %copy-done.17, bf16[3,384]{1,0:T(4,128)(2,1)S(1)} %copy-done.16, bf16[3,384]{1,0:T(4,128)(2,1)S(1)} %copy-done.18), kind=kOutput, calls=%fused_computation.5 | convolution fusion | flops 59789568 | bytes 334592 | tf_op jit(solution)/shard_map/while/body/eval_jaxpr/pr,mr->pm/dot_general | solution.py:136
  53.4 0.8 slice_bitcast_fusion.2
  54.2 0.8 slice_bitcast_fusion.3
  55.1 3.6 %fusion.12 = bf16[8192,128]{1,0:T(8,128)(2,1)S(1)} fusion(s32[8192]{0:T(1024)} %bitcast.295, bf16[128,128]{1,0:T(8,128)(2,1)S(1)} %get-tuple-element.128, bf16[128,128]{1,0:T(8,128)(2,1)S(1)} %get-tuple-element.124, bf16[128,128]{1,0:T(8,128)(2,1)S(1)} %copy-done.11), kind=kOutput, calls=%fused_computation.13 | convolution fusion | flops 809795584 | bytes 2228224 | tf_op jit(solution)/shard_map/while/body/eval_jaxpr/dot_general | solution.py:132
  58.7 1.8 %fusion.32 = f32[16,64,128]{1,0,2:T(8,128)S(1)} fusion(bf16[64,128,128]{2,1,0:T(8,128)(2,1)S(1)} %bitcast.257, bf16[128,16,128]{2,0,1:T(8,128)(2,1)S(1)} %pad_maximum_fusion), kind=kOutput, calls=%fused_computation.33 | convolution fusion | flops 33554432 | bytes 3145728 | tf_op jit(solution)/shard_map/while/body/eval_jaxpr/kac,aec->eka/dot_general | solution.py:142
  61.4 2.9 %fusion.13 = bf16[8192,128]{1,0:T(8,128)(2,1)S(1)} fusion(s32[8192]{0:T(1024)S(1)} %bitcast.299, bf16[128,128]{1,0:T(8,128)(2,1)S(1)} %get-tuple-element.127, bf16[128,128]{1,0:T(8,128)(2,1)S(1)} %get-tuple-element.123, bf16[128,128]{1,0:T(8,128)(2,1)S(1)} %copy-done.10), kind=kOutput, calls=%fused_computation.14 | convolution fusion | flops 809795584 | bytes 2228224 | tf_op jit(solution)/shard_map/while/body/eval_jaxpr/dot_general | solution.py:132
  64.3 1.8 %fusion.35 = f32[16,64,128]{1,0,2:T(8,128)S(1)} fusion(bf16[64,128,128]{2,1,0:T(8,128)(2,1)S(1)} %bitcast.258, bf16[128,16,128]{2,0,1:T(8,128)(2,1)S(1)} %pad_maximum_fusion.1), kind=kOutput, calls=%fused_computation.34 | convolution fusion | flops 33554432 | bytes 3145728 | tf_op jit(solution)/shard_map/while/body/eval_jaxpr/kac,aec->eka/dot_general | solution.py:142
  66.9 3.1 %fusion.14 = bf16[8192,128]{1,0:T(8,128)(2,1)S(1)} fusion(s32[8192]{0:T(1024)S(1)} %bitcast.300, bf16[128,128]{1,0:T(8,128)(2,1)S(1)} %get-tuple-element.125, bf16[128,128]{1,0:T(8,128)(2,1)S(1)} %get-tuple-element.121, bf16[128,128]{1,0:T(8,128)(2,1)S(1)} %copy-done.9), kind=kOutput, calls=%fused_computation.15 | convolution fusion | flops 809795584 | bytes 2228224 | tf_op jit(solution)/shard_map/while/body/eval_jaxpr/dot_general | solution.py:132
  70.0 1.8 %fusion.38 = f32[16,64,128]{1,0,2:T(8,128)S(1)} fusion(bf16[64,128,128]{2,1,0:T(8,128)(2,1)S(1)} %bitcast.259, bf16[128,16,128]{2,0,1:T(8,128)(2,1)S(1)} %pad_maximum_fusion.2), kind=kOutput, calls=%fused_computation.35 | convolution fusion | flops 33554432 | bytes 3145728 | tf_op jit(solution)/shard_map/while/body/eval_jaxpr/kac,aec->eka/dot_general | solution.py:142
  72.6 2.9 %fusion.15 = bf16[8192,128]{1,0:T(8,128)(2,1)S(1)} fusion(s32[8192]{0:T(1024)S(1)} %bitcast.301, bf16[128,128]{1,0:T(8,128)(2,1)S(1)} %get-tuple-element.126, bf16[128,128]{1,0:T(8,128)(2,1)S(1)} %get-tuple-element.122, bf16[128,128]{1,0:T(8,128)(2,1)S(1)} %copy-done.8), kind=kOutput, calls=%fused_computation.16 | convolution fusion | flops 809795584 | bytes 2228224 | tf_op jit(solution)/shard_map/while/body/eval_jaxpr/dot_general | solution.py:132
  75.5 1.8 %fusion.41 = f32[16,64,128]{1,0,2:T(8,128)S(1)} fusion(bf16[64,128,128]{2,1,0:T(8,128)(2,1)S(1)} %bitcast.260, bf16[128,16,128]{2,0,1:T(8,128)(2,1)S(1)} %pad_maximum_fusion.3), kind=kOutput, calls=%fused_computation.36 | convolution fusion | flops 33554432 | bytes 3145728 | tf_op jit(solution)/shard_map/while/body/eval_jaxpr/kac,aec->eka/dot_general | solution.py:142
  78.3 4.4 %all_gather.6 = f32[2,8,3,128]{3,0,2,1:T(2,128)S(1)} all-gather(f32[2,4,3,128]{3,0,2,1:T(2,128)S(1)} %copy.182), channel_id=1, replica_groups=mesh['space'=16,'bead'=2] {'bead'}, dimensions={1}, use_global_device_ids=true | all-gather | bytes 36864 | tf_op jit(solution)/shard_map/all_gather | solution.py:223
  83.1 4.4 %all_gather.7 = f32[2,8,3,128]{3,0,2,1:T(2,128)S(1)} all-gather(f32[2,4,3,128]{3,0,2,1:T(2,128)S(1)} %copy.184), channel_id=1, replica_groups=mesh['space'=16,'bead'=2] {'bead'}, dimensions={1}, use_global_device_ids=true | all-gather | bytes 36864 | tf_op jit(solution)/shard_map/all_gather | solution.py:231
  (140 shorter events, 23.1 us)
Async XLA Ops:
  0.6 23.4 %copy-start = (bf16[4,128,128]{2,1,0:T(8,128)(2,1)S(1)}, bf16[4,128,128]{2,1,0:T(8,128)(2,1)}, u32[]{:S(2)}) copy-start(bf16[4,128,128]{2,1,0:T(8,128)(2,1)} %param.15) | copy-start | bytes 393220
  0.6 26.1 %copy-start.5 = (s32[64,128]{1,0:T(8,128)S(1)}, s32[64,128]{1,0:T(8,128)}, u32[]{:S(2)}) copy-start(s32[64,128]{1,0:T(8,128)} %param.17) | copy-start | bytes 98308
  0.7 27.5 %copy-start.6 = (bf16[128,128]{1,0:T(8,128)(2,1)S(1)}, bf16[128,128]{1,0:T(8,128)(2,1)}, u32[]{:S(2)}) copy-start(bf16[128,128]{1,0:T(8,128)(2,1)} %param.21) | copy-start | bytes 98308
  0.7 27.6 %copy-start.7 = (bf16[128,128]{1,0:T(8,128)(2,1)S(1)}, bf16[128,128]{1,0:T(8,128)(2,1)}, u32[]{:S(2)}) copy-start(bf16[128,128]{1,0:T(8,128)(2,1)} %param.20) | copy-start | bytes 98308
  3.0 33.8 %collective-permute-start.3 = (f32[4,3,128]{2,0,1:T(4,128)}, f32[4,3,128]{2,0,1:T(4,128)}, u32[]{:S(2)}, u32[]{:S(2)}) collective-permute-start(f32[4,3,128]{2,0,1:T(4,128)} %get-tuple-element.149), channel_id=1, source_target_pairs={{2,0},{4,2},{6,4},{8,6},{10,8},{12,10},{14,12},{16,14},{18,16},{20... | collective-permute-start | bytes 18440 | tf_op jit(solution)/shard_map/ppermute | solution.py:20
  9.0 28.6 %collective-permute-start.2 = (f32[4,3,128]{2,1,0:T(4,128)}, f32[4,3,128]{2,1,0:T(4,128)}, u32[]{:S(2)}, u32[]{:S(2)}) collective-permute-start(f32[4,3,128]{2,1,0:T(4,128)} %copy.192), channel_id=1, source_target_pairs={{0,2},{2,4},{4,6},{6,8},{8,10},{10,12},{12,14},{14,16},{16,18},{18... | collective-permute-start | bytes 18440 | tf_op jit(solution)/shard_map/ppermute | solution.py:17
  10.9 42.5 %collective-permute-start.1 = (bf16[4,128,128]{2,1,0:T(8,128)(2,1)}, bf16[4,128,128]{2,1,0:T(8,128)(2,1)}, u32[]{:S(2)}, u32[]{:S(2)}) collective-permute-start(bf16[4,128,128]{2,1,0:T(8,128)(2,1)} %get-tuple-element.106), channel_id=1, source_target_pairs={{2,0},{4,2},{6,4},{8,6},{10,8},{12,10},{14,12},{16,14},{18,16},{20... | collective-permute-start | bytes 393224 | tf_op jit(solution)/shard_map/ppermute | solution.py:20
  15.3 38.9 %collective-permute-start = (bf16[4,128,128]{2,1,0:T(8,128)(2,1)}, bf16[4,128,128]{2,1,0:T(8,128)(2,1)}, u32[]{:S(2)}, u32[]{:S(2)}) collective-permute-start(bf16[4,128,128]{2,1,0:T(8,128)(2,1)} %get-tuple-element.105), channel_id=1, source_target_pairs={{0,2},{2,4},{4,6},{6,8},{8,10},{10,12},{12,14},{14,16},{16,18},{18... | collective-permute-start | bytes 393224 | tf_op jit(solution)/shard_map/ppermute | solution.py:17
  23.1 11.4 %copy-start.19 = (f32[128]{0:T(128)S(1)}, f32[128]{0:T(128)}, u32[]{:S(2)}) copy-start(f32[128]{0:T(128)} %param.14) | copy-start | bytes 1540
  35.1 5.6 %copy-start.23 = (s32[64,128]{1,0:T(8,128)S(1)}, s32[64,128]{1,0:T(8,128)}, u32[]{:S(2)}) copy-start(s32[64,128]{1,0:T(8,128)} %param.16) | copy-start | bytes 98308
  43.0 2.3 %copy-start.1 = (f32[1,3,64,128]{3,2,1,0:T(8,128)S(1)}, f32[1,3,64,128]{3,2,1,0:T(8,128)}, u32[]{:S(2)}) copy-start(f32[1,3,64,128]{3,2,1,0:T(8,128)} %broadcast_bitcast_fusion.2) | copy-start | bytes 294916
  45.7 4.7 %copy-start.16 = (bf16[3,384]{1,0:T(4,128)(2,1)S(1)}, bf16[3,384]{1,0:T(4,128)(2,1)}, u32[]{:S(2)}) copy-start(bf16[3,384]{1,0:T(4,128)(2,1)} %get-tuple-element.178) | copy-start | bytes 6916
  45.8 4.7 %copy-start.17 = (bf16[3,384]{1,0:T(4,128)(2,1)S(1)}, bf16[3,384]{1,0:T(4,128)(2,1)}, u32[]{:S(2)}) copy-start(bf16[3,384]{1,0:T(4,128)(2,1)} %get-tuple-element.179) | copy-start | bytes 6916
  45.8 4.7 %copy-start.18 = (bf16[3,384]{1,0:T(4,128)(2,1)S(1)}, bf16[3,384]{1,0:T(4,128)(2,1)}, u32[]{:S(2)}) copy-start(bf16[3,384]{1,0:T(4,128)(2,1)} %fusion.244) | copy-start | bytes 6916
  45.8 4.7 %copy-start.24 = (s32[64,128]{1,0:T(8,128)S(1)}, s32[64,128]{1,0:T(8,128)}, u32[]{:S(2)}) copy-start(s32[64,128]{1,0:T(8,128)} %param.16) | copy-start | bytes 98308
  50.5 4.6 %copy-start.11 = (bf16[128,128]{1,0:T(8,128)(2,1)S(1)}, bf16[128,128]{1,0:T(8,128)(2,1)}, u32[]{:S(2)}) copy-start(bf16[128,128]{1,0:T(8,128)(2,1)} %get-tuple-element.109) | copy-start | bytes 98308
  58.7 1.9 %copy-start.4 = (f32[64,128]{0,1:T(8,128)S(1)}, f32[64,128]{0,1:T(8,128)}, u32[]{:S(2)}) copy-start(f32[64,128]{0,1:T(8,128)} %copy.159) | copy-start | bytes 98308
  58.7 1.9 %copy-start.26 = (f32[8]{0:T(128)S(1)}, f32[8]{0:T(128)}, u32[]{:S(2)}) copy-start(f32[8]{0:T(128)} %param.23) | copy-start | bytes 100
  60.6 0.8 copy-start.10
  60.6 0.8 copy-start.25
  64.3 1.9 %copy-start.3 = (f32[64,128]{0,1:T(8,128)S(1)}, f32[64,128]{0,1:T(8,128)}, u32[]{:S(2)}) copy-start(f32[64,128]{0,1:T(8,128)} %copy.165) | copy-start | bytes 98308
  66.1 0.8 copy-start.9
  71.9 0.8 copy-start.8
  77.4 0.8 copy-start.2
  77.4 0.9 %copy-start.15 = (f32[4,3,128]{2,0,1:T(4,128)S(1)}, f32[4,3,128]{2,0,1:T(4,128)}, u32[]{:S(2)}) copy-start(f32[4,3,128]{2,0,1:T(4,128)} %param.13) | copy-start | bytes 18436
  77.4 0.9 %copy-start.12 = (f32[4,3,128]{2,0,1:T(4,128)S(1)}, f32[4,3,128]{2,0,1:T(4,128)}, u32[]{:S(2)}) copy-start(f32[4,3,128]{2,0,1:T(4,128)} %param.12) | copy-start | bytes 18436
  77.4 5.4 %copy-start.13 = (f32[8,8]{0,1:T(8,128)S(1)}, f32[8,8]{0,1:T(8,128)}, u32[]{:S(2)}) copy-start(f32[8,8]{0,1:T(8,128)} %fusion.213) | copy-start | bytes 772
  77.4 5.5 %copy-start.14 = (f32[4,128]{1,0:T(4,128)S(1)}, f32[4,128]{1,0:T(4,128)}, u32[]{:S(2)}) copy-start(f32[4,128]{1,0:T(4,128)} %multiply_multiply_fusion.2) | copy-start | bytes 6148
  77.4 5.5 %copy-start.20 = (f32[128]{0:T(128)S(1)}, f32[128]{0:T(128)}, u32[]{:S(2)}) copy-start(f32[128]{0:T(128)} %param.14) | copy-start | bytes 1540
  77.4 5.5 %copy-start.21 = (f32[4]{0:T(128)S(1)}, f32[4]{0:T(128)}, u32[]{:S(2)}) copy-start(f32[4]{0:T(128)} %get-tuple-element.89) | copy-start | bytes 52
  77.4 5.5 %copy-start.22 = (f32[4]{0:T(128)S(1)}, f32[4]{0:T(128)}, u32[]{:S(2)}) copy-start(f32[4]{0:T(128)} %compare_select_fusion) | copy-start | bytes 52
where the time goes:
time: 89.8 us; the launch traced here: 88.4 us
  matrix products  42.2 us (47%)
  local copies, waits for them, and re-layouts  15.2 us (17%)
  other arithmetic  10.9 us (12%)
  starting transfers between devices  9.89 us (11%)
  blocking collectives  8.8 us (10%)
  between operations  1.34 us (1%)
    dot_general x4, matrix products, one_block(): jnp.dot(selector, feature_table, preferred_element_type=jnp.float32)  12.6 us
    dot_general x4, matrix products, one_block(): jnp.einsum('pr,mr->pm', coordinate_pieces, selector, preferred_element_ty...  10 us
    ppermute x2, starting transfers between devices, padded(): lax.ppermute(lax.slice_in_dim(block, 0, width, axis=dim), axis, backward)  9.88 us
    dot_general x4, matrix products, one_block(): jnp.einsum('kac,aec->eka', gathered, probe_mats, preferred_element_type=j...  7.38 us
    unnamed x63, local copies, waits for them, and re-layouts  4.41 us
    all_gather x1, blocking collectives, body(): lax.all_gather(stacked, 'bead', axis=1, tiled=True)  4.4 us
    all_gather x1, blocking collectives, body(): lax.all_gather(jnp.stack([next_pos, next_mom]), 'bead', axis=1, tiled=True)  4.4 us
    dot_general x4, matrix products, probe_matrices(): jnp.dot(own_features, w_probe, preferred_element_type=jnp.float32)  2.89 us
  transfers between devices with their start and end apart: 4, of which 0 were waited for; matrix products, arithmetic and copies ran while one was open for 46% of the time, Pallas kernels for 0%

commit v1 on v0

v1 whole, which is shorter than its diff:
```python
import functools
import math

import jax
import jax.numpy as jnp
import numpy as np
from jax import lax
from jax.experimental import pallas as pl
from jax.experimental.pallas import tpu as pltpu
from jax.sharding import PartitionSpec as P

STIFFNESS = 1.3
BOX_LENGTH = 2.0
SCORE_CAP = 30.0
ROWS = 8
F32 = jnp.float32
BF16 = jnp.bfloat16
NT = (((1,), (1,)), ((), ()))


def step_tables(beads):
    modes = np.arange(beads)
    turn = 2.0 * STIFFNESS * np.sin(np.pi * modes / beads)
    safe = np.where(turn > 0, turn, 1.0)
    gain = np.where(turn > 0, np.sin(turn) / safe, 1.0)
    waves = np.cos(2.0 * np.pi * np.outer(modes, modes) / beads) / beads
    return waves @ np.cos(turn), waves @ gain, waves @ (turn * np.sin(turn))


def pick(table, index):
    return jnp.take_along_axis(table, index, axis=1, mode="promise_in_bounds")


def split_two(value):
    high = value.astype(BF16)
    return jnp.concatenate([high, (value - high.astype(F32)).astype(BF16)], axis=1)


def step_kernel(
    n_space, n_bead,
    pos, mom, mass, feat, near, image, face, w_query, w_key, w_value, w_probe, rate,
    new_pos, new_mom,
    feat_halo, pos_halo, face_halo, peer_pos, peer_kick, kick,
    probes, dots_own, dots_halo, first, index_t, low_t, shift_t, own_t, offs, weights, scaled,
    feat_send, feat_recv, pos_send, pos_recv, face_send, face_recv,
    peer_send, peer_recv, kick_send, kick_recv,
):
    beads, atoms, channels = feat.shape
    near_count = near.shape[0]
    heads = rate.shape[0]
    head_size = channels // heads
    pairs = beads // 2
    terms = 2 * heads
    s = lax.axis_index("space")
    g = lax.axis_index("bead")
    upper = lax.rem(s + 1, n_space)
    lower = lax.rem(s + n_space - 1, n_space)
    peers = [lax.rem(g + r, n_bead) for r in range(1, n_bead)]

    def copy(src, dst, send, recv, target):
        return pltpu.make_async_remote_copy(
            src_ref=src, dst_ref=dst, send_sem=send, recv_sem=recv,
            device_id=target, device_id_type=pl.DeviceIdType.MESH,
        )

    barrier = pltpu.get_barrier_semaphore()
    for target in [(lower, g), (upper, g)] + [(s, q) for q in peers]:
        pl.semaphore_signal(barrier, inc=1, device_id=target, device_id_type=pl.DeviceIdType.MESH)
    pl.semaphore_wait(barrier, 2 + len(peers))

    sides = [(0, (upper, g)), (1, (lower, g))]
    face_copies = [
        copy(face.at[1 - slot], face_halo.at[slot], face_send.at[slot], face_recv.at[slot], to)
        for slot, to in sides
    ]
    pos_copies = [
        copy(pos, pos_halo.at[slot], pos_send.at[slot], pos_recv.at[slot], to) for slot, to in sides
    ]
    feat_copies = [
        [
            copy(feat.at[b], feat_halo.at[slot, b], feat_send.at[slot, b], feat_recv.at[slot, b], to)
            for slot, to in sides
        ]
        for b in range(beads)
    ]
    peer_copies = [
        copy(pos, peer_pos.at[n_bead - r - 2], peer_send.at[r], peer_recv.at[n_bead - r - 2], (s, q))
        for r, q in enumerate(peers)
    ]
    for c in face_copies + pos_copies:
        c.start()
    for both in feat_copies:
        for c in both:
            c.start()
    for c in peer_copies:
        c.start()

    near2 = jnp.concatenate([near[...], near[...]], axis=0)
    index = jnp.transpose(near2)
    index_t[...] = index
    low_t[...] = jnp.bitwise_and(index, atoms - 1)
    code = image[...]
    one = lambda test: jnp.where(test, 1, 0)
    z = one(code >= 9) + one(code >= 18)
    rest = code - 9 * z
    y = one(rest >= 3) + one(rest >= 6)
    x = rest - 3 * y
    for c, part in enumerate((x, y, z)):
        shift = BOX_LENGTH * (part.astype(F32) - 1.0)
        shift_t[c] = jnp.transpose(jnp.concatenate([shift, shift], axis=0))
    for b in range(beads):
        padded = jnp.concatenate([pos[b], jnp.zeros((5, atoms), F32)], axis=0)
        own_t[b] = jnp.transpose(padded)

    flat = feat[...].reshape(beads * atoms, channels)
    depth_head = lax.broadcasted_iota(jnp.int32, (channels, channels), 0) // head_size
    for kind, (into, out) in enumerate(((w_query, w_key), (w_probe, w_value))):
        small = split_two(jnp.dot(flat, into[...], preferred_element_type=F32))
        turned = jnp.transpose(out[...].astype(F32))
        wide = jnp.concatenate(
            [jnp.where(depth_head == h, turned, 0.0).astype(BF16) for h in range(heads)], axis=1
        )
        full = jnp.dot(small, jnp.concatenate([wide, wide], axis=0), preferred_element_type=F32)
        full = full.astype(BF16)
        for b in range(beads):
            for h in range(heads):
                probes[b, kind * heads + h] = full[
                    b * atoms : (b + 1) * atoms, h * channels : (h + 1) * channels
                ]

    half = lax.broadcasted_iota(jnp.int32, (ROWS, 2 * near_count), 1) < near_count
    chunks = atoms // ROWS

    for b in range(beads):
        dots_own[b] = lax.dot_general(
            probes[b].reshape(terms * atoms, channels), feat[b], NT, preferred_element_type=F32
        ).reshape(terms, atoms, atoms)

    def pick_own(i, carry):
        rows = pl.ds(pl.multiple_of(i * ROWS, ROWS), ROWS)
        low = low_t[rows, :]
        for p in range(pairs):
            for e in range(terms):
                a = pick(dots_own[2 * p, e, rows, :], low)
                b = pick(dots_own[2 * p + 1, e, rows, :], low)
                first[p, e, rows, :] = jnp.where(half, a, b)
        return carry

    lax.fori_loop(0, chunks, pick_own, 0)

    for c in face_copies:
        c.wait_recv()

    def remap(i, carry):
        rows = pl.ds(pl.multiple_of(i * ROWS, ROWS), ROWS)
        low = low_t[rows, :]
        full = index_t[rows, :]
        from_lower = pick(jnp.broadcast_to(face_halo[0], (ROWS, atoms)), low)
        from_upper = pick(jnp.broadcast_to(face_halo[1], (ROWS, atoms)), low)
        low_t[rows, :] = jnp.where(
            full < atoms, low, jnp.where(full < 2 * atoms, from_lower, from_upper)
        )
        return carry

    lax.fori_loop(0, chunks, remap, 0)

    for c in pos_copies:
        c.wait_recv()

    def place(i, carry):
        rows = pl.ds(pl.multiple_of(i * ROWS, ROWS), ROWS)
        low = low_t[rows, :]
        full = index_t[rows, :]
        is_own = full < atoms
        is_lower = full < 2 * atoms
        for p in range(pairs):
            for c in range(3):
                found = []
                mine = []
                for b in (2 * p, 2 * p + 1):
                    line = [
                        pick(jnp.broadcast_to(r, (ROWS, atoms)), low)
                        for r in (
                            pos[b, c : c + 1, :],
                            pos_halo[0, b, c : c + 1, :],
                            pos_halo[1, b, c : c + 1, :],
                        )
                    ]
                    found.append(jnp.where(is_own, line[0], jnp.where(is_lower, line[1], line[2])))
                    mine.append(
                        jnp.broadcast_to(own_t[b, rows, c : c + 1], (ROWS, 2 * near_count))
                    )
                gap = jnp.where(half, found[0], found[1]) - jnp.where(half, mine[0], mine[1])
                offs[p, c, rows, :] = gap + shift_t[c, rows, :]
        return carry

    lax.fori_loop(0, chunks, place, 0)

    log2e = math.log2(math.e)
    sum_row = lax.broadcasted_iota(jnp.int32, (4 * near_count, 2 * near_count), 0)
    sum_col = lax.broadcasted_iota(jnp.int32, (4 * near_count, 2 * near_count), 1)
    same_half = (jnp.bitwise_and(sum_row, near_count) > 0) == (sum_col >= near_count)
    sum_table = jnp.where(same_half, 1.0, 0.0).astype(BF16)
    pick_row = lax.broadcasted_iota(jnp.int32, (8, 2 * near_count), 0)
    pick_col = lax.broadcasted_iota(jnp.int32, (8, 2 * near_count), 1)
    in_half = (pick_row == 0) == (pick_col < near_count)
    half_table = jnp.where(in_half & (pick_row < 2), 1.0, 0.0)
    kick_copies = []

    for p in range(pairs):
        for b in (2 * p, 2 * p + 1):
            for c in feat_copies[b]:
                c.wait_recv()
            table = jnp.concatenate([feat_halo[0, b], feat_halo[1, b]], axis=0)
            dots_halo[b] = lax.dot_general(
                probes[b].reshape(terms * atoms, channels), table, NT, preferred_element_type=F32
            ).reshape(terms, atoms, 2 * atoms)

        def attend(i, carry):
            rows = pl.ds(pl.multiple_of(i * ROWS, ROWS), ROWS)
            low = low_t[rows, :]
            full = index_t[rows, :]
            is_own = full < atoms
            is_lower = full < 2 * atoms
            off = [offs[p, c, rows, :] for c in range(3)]
            distance = off[0] * off[0] + off[1] * off[1] + off[2] * off[2]

            def term(e):
                found = []
                for b in (2 * p, 2 * p + 1):
                    a = pick(dots_halo[b, e, rows, 0:atoms], low)
                    c = pick(dots_halo[b, e, rows, atoms : 2 * atoms], low)
                    found.append(jnp.where(is_lower, a, c))
                return jnp.where(is_own, first[p, e, rows, :], jnp.where(half, found[0], found[1]))

            for h in range(heads):
                capped = jnp.tanh(term(h) * (1.0 / (SCORE_CAP * head_size**0.5)))
                weight = jnp.exp2(
                    capped * (SCORE_CAP * log2e) - distance * (rate[h] * log2e)
                )
                weights[h, rows, :] = weight
                scaled[h, rows, :] = weight * term(heads + h)
            return carry

        lax.fori_loop(0, chunks, attend, 0)

        totals = jnp.dot(
            split_two(weights[...].reshape(heads * atoms, 2 * near_count)),
            sum_table,
            preferred_element_type=F32,
        ).reshape(heads, atoms, 2 * near_count)
        coupling = scaled[0] / totals[0]
        for h in range(1, heads):
            coupling = coupling + scaled[h] / totals[h]
        for c in range(3):
            force = lax.dot_general(
                half_table, coupling * offs[p, c], NT,
                precision=lax.Precision.HIGHEST, preferred_element_type=F32,
            ) * (1.0 / (heads * head_size**0.5))
            for j in range(2):
                b = 2 * p + j
                kick[b, c : c + 1, :] = mom[b, c : c + 1, :] + force[j : j + 1, :]
        for r, q in enumerate(peers):
            c = copy(
                kick.at[pl.ds(2 * p, 2)],
                peer_kick.at[n_bead - r - 2, pl.ds(2 * p, 2)],
                kick_send.at[r, p],
                kick_recv.at[n_bead - r - 2, p],
                (s, q),
            )
            c.start()
            kick_copies.append(c)

    total = beads * n_bead
    keep, gain, pull = step_tables(total)
    for c in peer_copies + kick_copies:
        c.wait_recv()
    weight = mass[...]
    inverse = 1.0 / weight
    for b in range(beads):
        kept_pos = moved = kept_mom = pulled = None
        for q in range(n_bead):
            for j in range(beads):
                where_pos = pos[j] if q == 0 else peer_pos[q - 1, j]
                where_kick = kick[j] if q == 0 else peer_kick[q - 1, j]
                d = (b - j - q * beads) % total
                parts = (
                    where_pos * float(keep[d]),
                    where_kick * float(gain[d]),
                    where_kick * float(keep[d]),
                    where_pos * float(pull[d]),
                )
                if kept_pos is None:
                    kept_pos, moved, kept_mom, pulled = parts
                else:
                    kept_pos = kept_pos + parts[0]
                    moved = moved + parts[1]
                    kept_mom = kept_mom + parts[2]
                    pulled = pulled + parts[3]
        new_pos[b] = kept_pos + moved * inverse
        new_mom[b] = kept_mom - weight * pulled

    for c in face_copies + pos_copies + peer_copies + kick_copies:
        c.wait_send()
    for both in feat_copies:
        for c in both:
            c.wait_send()


def body(
    n_space, n_bead,
    positions, momenta, masses, features, neighbours, images, face_map,
    w_query, w_key, w_value, w_probe, radial_rate,
):
    beads, atoms, channels = features.shape
    heads = radial_rate.shape[0]
    near = neighbours.shape[0]
    terms = 2 * heads
    pairs = beads // 2
    wide = 2 * near
    peers = n_bead - 1
    vmem = pl.BlockSpec(memory_space=pltpu.VMEM)
    smem = pl.BlockSpec(memory_space=pltpu.SMEM)
    dma = pltpu.SemaphoreType.DMA
    shape = jax.ShapeDtypeStruct(positions.shape, F32)
    return pl.pallas_call(
        functools.partial(step_kernel, n_space, n_bead),
        out_shape=(shape, shape),
        in_specs=[vmem] * 11 + [smem],
        out_specs=(vmem, vmem),
        scratch_shapes=[
            pltpu.VMEM((2, beads, atoms, channels), BF16),
            pltpu.VMEM((2, beads, 3, atoms), F32),
            pltpu.VMEM((2, 1, atoms), jnp.int32),
            pltpu.VMEM((peers, beads, 3, atoms), F32),
            pltpu.VMEM((peers, beads, 3, atoms), F32),
            pltpu.VMEM((beads, 3, atoms), F32),
            pltpu.VMEM((beads, terms, atoms, channels), BF16),
            pltpu.VMEM((beads, terms, atoms, atoms), F32),
            pltpu.VMEM((beads, terms, atoms, 2 * atoms), F32),
            pltpu.VMEM((pairs, terms, atoms, wide), F32),
            pltpu.VMEM((atoms, wide), jnp.int32),
            pltpu.VMEM((atoms, wide), jnp.int32),
            pltpu.VMEM((3, atoms, wide), F32),
            pltpu.VMEM((beads, atoms, 8), F32),
            pltpu.VMEM((pairs, 3, atoms, wide), F32),
            pltpu.VMEM((heads, atoms, wide), F32),
            pltpu.VMEM((heads, atoms, wide), F32),
            dma((2, beads)), dma((2, beads)), dma((2,)), dma((2,)), dma((2,)), dma((2,)),
            dma((peers,)), dma((peers,)), dma((peers, pairs)), dma((peers, pairs)),
        ],
        compiler_params=pltpu.CompilerParams(
            collective_id=0, has_side_effects=True, vmem_limit_bytes=50 * 2**20
        ),
    )(
        positions, momenta, masses.reshape(1, atoms), features, neighbours, images, face_map,
        w_query, w_key, w_value, w_probe, radial_rate,
    )


def solution(mesh):
    placed = (
        P("bead", None, "space"),
        P("bead", None, "space"),
        P("space"),
        P("bead", "space", None),
        P(None, "space"),
        P(None, "space"),
        P(None, "space", None),
        P(),
        P(),
        P(),
        P(),
        P(),
    )
    return jax.shard_map(
        functools.partial(body, mesh.shape["space"], mesh.shape["bead"]),
        mesh=mesh,
        in_specs=placed,
        out_specs=(P("bead", None, "space"), P("bead", None, "space")),
        check_vma=False,
    )
```

time: 89.8 us -> 35 us (0.39)
  matrix products: 42.2 us -> 0 us
  Pallas kernels: 0 us -> 25.7 us
  other arithmetic: 10.9 us -> 0 us
  starting transfers between devices: 9.89 us -> 0 us
  blocking collectives: 8.8 us -> 0 us
  local copies, waits for them, and re-layouts: 15.2 us -> 8.01 us
    dot_general x32 -> x0, matrix products: 42.2 us -> none  [the longest x4 12.6 us: one_block(): jnp.dot(selector, feature_table, preferred_element_type=jnp.float32)]
    pallas_call x0 -> x1, Pallas kernels: none -> 25.7 us  [body(): pl.pallas_call(functools.partial(step_kernel, n_space, n_bead), out_shape...]
    ppermute x4 -> x0, starting transfers between devices: 9.89 us -> none  [the longest x2 9.88 us: padded(): lax.ppermute(lax.slice_in_dim(block, 0, width, axis=dim), axis, backward)]
    all_gather x2 -> x0, blocking collectives: 8.8 us -> none  [the longest x1 4.4 us: body(): lax.all_gather(stacked, 'bead', axis=1, tiled=True)]
    squeeze x10 -> x0, local copies, waits for them, and re-layouts: 5.16 us -> none  [the longest x1 1.48 us: body(): features[bead_slot]]
    slice x4 -> x0, local copies, waits for them, and re-layouts: 3.03 us -> none  [the longest x2 1.34 us: padded(): lax.slice_in_dim(block, block.shape[dim] - width, None, axis=dim)]
    convert_element_type x9 -> x0, other arithmetic: 3.03 us -> none  [the longest x4 1.22 us: split_pieces(): middle_part = first_rest.astype(jnp.bfloat16)]
    unnamed x63 -> x24, local copies, waits for them, and re-layouts: 4.41 us -> 6.82 us
  transfers between devices with their start and end apart: 4 -> 0, of which waited for: 0 -> 0; matrix products, arithmetic and copies ran while one was open for 46% -> 0% of each run, Pallas kernels for 0% -> 0%
where the time goes in v1:
time: 35 us; the launch traced here: 34.4 us
  Pallas kernels  25.7 us (73%)
  local copies, waits for them, and re-layouts  8.01 us (23%)
  between operations  0.68 us (2%)
    pallas_call x1, Pallas kernels, body(): pl.pallas_call(functools.partial(step_kernel, n_space, n_bead), out_shape...  25.7 us
    unnamed x24, local copies, waits for them, and re-layouts  6.82 us
    pallas_call x2, local copies, waits for them, and re-layouts, body(): pl.pallas_call(functools.partial(step_kernel, n_space, n_bead), out_shape...  1.19 us

profile of v1, /device:TPU:0, one launch (start us, length us, event | category | flops | bytes accessed | tf_op | source)
XLA Modules:
  0.0 34.4 jit_solution(8154703053358049794)
XLA Ops:
  0.6 0.0 copy-start.10
  0.6 0.7 %copy.14.pos = f32[4,3,128]{2,1,0:T(4,128)S(1)} copy(f32[4,3,128]{2,0,1:T(4,128)} %param.12) | data formatting | bytes 12288 | tf_op args[0]
  1.3 0.0 copy-done.10
  1.3 0.0 copy-start.7
  1.3 0.0 copy-start.8
  1.3 0.0 copy-start.9
  1.4 0.6 %copy-done.7 = s32[2,1,128]{2,1,0:T(1,128)S(1)} copy-done((s32[2,1,128]{2,1,0:T(1,128)S(1)}, s32[2,1,128]{2,1,0:T(1,128)}, u32[]{:S(2)}) %copy-start.7) | copy-done | bytes 1048
  2.0 0.0 copy-done.8
  2.0 0.0 copy-done.9
  2.0 0.0 copy-start
  2.0 0.9 %copy-done = bf16[4,128,128]{2,1,0:T(8,128)(2,1)S(1)} copy-done((bf16[4,128,128]{2,1,0:T(8,128)(2,1)S(1)}, bf16[4,128,128]{2,1,0:T(8,128)(2,1)}, u32[]{:S(2)}) %copy-start) | copy-done | bytes 131096
  2.9 0.0 copy-start.1
  2.9 0.8 %copy-done.1 = s32[64,128]{1,0:T(8,128)S(1)} copy-done((s32[64,128]{1,0:T(8,128)S(1)}, s32[64,128]{1,0:T(8,128)}, u32[]{:S(2)}) %copy-start.1) | copy-done | bytes 32792
  3.7 0.0 copy-start.2
  3.7 0.8 %copy-done.2 = s32[64,128]{1,0:T(8,128)S(1)} copy-done((s32[64,128]{1,0:T(8,128)S(1)}, s32[64,128]{1,0:T(8,128)}, u32[]{:S(2)}) %copy-start.2) | copy-done | bytes 32792
  4.5 0.0 copy-start.3
  4.5 0.8 %copy-done.3 = bf16[128,128]{1,0:T(8,128)(2,1)S(1)} copy-done((bf16[128,128]{1,0:T(8,128)(2,1)S(1)}, bf16[128,128]{1,0:T(8,128)(2,1)}, u32[]{:S(2)}) %copy-start.3) | copy-done | bytes 32792
  5.2 0.0 copy-start.4
  5.2 0.8 %copy-done.4 = bf16[128,128]{1,0:T(8,128)(2,1)S(1)} copy-done((bf16[128,128]{1,0:T(8,128)(2,1)S(1)}, bf16[128,128]{1,0:T(8,128)(2,1)}, u32[]{:S(2)}) %copy-start.4) | copy-done | bytes 32792
  6.0 0.0 copy-start.5
  6.0 0.8 %copy-done.5 = bf16[128,128]{1,0:T(8,128)(2,1)S(1)} copy-done((bf16[128,128]{1,0:T(8,128)(2,1)S(1)}, bf16[128,128]{1,0:T(8,128)(2,1)}, u32[]{:S(2)}) %copy-start.5) | copy-done | bytes 32792
  6.7 0.0 copy-start.6
  6.7 0.8 %copy-done.6 = bf16[128,128]{1,0:T(8,128)(2,1)S(1)} copy-done((bf16[128,128]{1,0:T(8,128)(2,1)S(1)}, bf16[128,128]{1,0:T(8,128)(2,1)}, u32[]{:S(2)}) %copy-start.6) | copy-done | bytes 32792
  7.5 25.7 %shard_map.131 = (f32[4,3,128]{2,1,0:T(4,128)S(1)}, f32[4,3,128]{2,1,0:T(4,128)S(1)}) custom-call(f32[4,3,128]{2,1,0:T(4,128)S(1)} %copy.14.pos, f32[4,3,128]{2,1,0:T(4,128)S(1)} %copy.15.mom, f32[1,128]{1,0:T(1,128)S(1)} %bitcast.1, bf16[4,128,128]{2,1,0:T(8,128)(2,1)S(1)} %copy-done, s32[64,128]{1,0:T(8,128)S(1)} %copy-done.1, s32[64,128]{1,0:T(8,128)S(1)} %copy-done.2, ...), custom_call_target="tpu_custom_call" | custom-call | tf_op jit(solution)/shard_map/pallas_call | solution.py:326
  33.2 0.6 %copy.16 = f32[4,3,128]{2,0,1:T(4,128)} copy(f32[4,3,128]{2,1,0:T(4,128)S(1)} %get-tuple-element.2) | data formatting | bytes 12288 | tf_op jit(solution)/shard_map/pallas_call | solution.py:326
  33.8 0.6 %copy.17 = f32[4,3,128]{2,0,1:T(4,128)} copy(f32[4,3,128]{2,1,0:T(4,128)S(1)} %get-tuple-element.3) | data formatting | bytes 12288 | tf_op jit(solution)/shard_map/pallas_call | solution.py:326
  (1 shorter events, 0.0 us)
Async XLA Ops:
  0.6 0.7 %copy-start.10 = (f32[4,3,128]{2,0,1:T(4,128)S(1)}, f32[4,3,128]{2,0,1:T(4,128)}, u32[]{:S(2)}) copy-start(f32[4,3,128]{2,0,1:T(4,128)} %param.13) | copy-start | bytes 18436
  1.3 0.7 %copy-start.7 = (s32[2,1,128]{2,1,0:T(1,128)S(1)}, s32[2,1,128]{2,1,0:T(1,128)}, u32[]{:S(2)}) copy-start(s32[2,1,128]{2,1,0:T(1,128)} %face.1) | copy-start | bytes 3076
  1.3 0.7 %copy-start.8 = (f32[128]{0:T(128)S(1)}, f32[128]{0:T(128)}, u32[]{:S(2)}) copy-start(f32[128]{0:T(128)} %param.14) | copy-start | bytes 1540
  1.3 0.7 %copy-start.9 = (f32[8]{0:T(128)S(1)}, f32[8]{0:T(128)}, u32[]{:S(2)}) copy-start(f32[8]{0:T(128)} %rate.1) | copy-start | bytes 100
  2.0 0.9 %copy-start = (bf16[4,128,128]{2,1,0:T(8,128)(2,1)S(1)}, bf16[4,128,128]{2,1,0:T(8,128)(2,1)}, u32[]{:S(2)}) copy-start(bf16[4,128,128]{2,1,0:T(8,128)(2,1)} %feat.1) | copy-start | bytes 393220
  2.9 0.8 %copy-start.1 = (s32[64,128]{1,0:T(8,128)S(1)}, s32[64,128]{1,0:T(8,128)}, u32[]{:S(2)}) copy-start(s32[64,128]{1,0:T(8,128)} %near.1) | copy-start | bytes 98308
  3.7 0.8 %copy-start.2 = (s32[64,128]{1,0:T(8,128)S(1)}, s32[64,128]{1,0:T(8,128)}, u32[]{:S(2)}) copy-start(s32[64,128]{1,0:T(8,128)} %image.1) | copy-start | bytes 98308
  4.5 0.8 %copy-start.3 = (bf16[128,128]{1,0:T(8,128)(2,1)S(1)}, bf16[128,128]{1,0:T(8,128)(2,1)}, u32[]{:S(2)}) copy-start(bf16[128,128]{1,0:T(8,128)(2,1)} %w_query.1) | copy-start | bytes 98308
  5.2 0.8 %copy-start.4 = (bf16[128,128]{1,0:T(8,128)(2,1)S(1)}, bf16[128,128]{1,0:T(8,128)(2,1)}, u32[]{:S(2)}) copy-start(bf16[128,128]{1,0:T(8,128)(2,1)} %w_key.1) | copy-start | bytes 98308
  6.0 0.8 %copy-start.5 = (bf16[128,128]{1,0:T(8,128)(2,1)S(1)}, bf16[128,128]{1,0:T(8,128)(2,1)}, u32[]{:S(2)}) copy-start(bf16[128,128]{1,0:T(8,128)(2,1)} %w_value.1) | copy-start | bytes 98308
  6.7 0.8 %copy-start.6 = (bf16[128,128]{1,0:T(8,128)(2,1)S(1)}, bf16[128,128]{1,0:T(8,128)(2,1)}, u32[]{:S(2)}) copy-start(bf16[128,128]{1,0:T(8,128)(2,1)} %w_probe.1) | copy-start | bytes 98308

commit v2 on v1

v2 whole, which is shorter than its diff:
```python
import functools
import math

import jax
import jax.numpy as jnp
import numpy as np
from jax import lax
from jax.experimental import pallas as pl
from jax.experimental.pallas import tpu as pltpu
from jax.sharding import PartitionSpec as P

STIFFNESS = 1.3
BOX_LENGTH = 2.0
SCORE_CAP = 30.0
ROWS = 16
VMEM_GRANT = 64 * 2**20 - 2**14
F32 = jnp.float32
BF16 = jnp.bfloat16
NT = (((1,), (1,)), ((), ()))


def step_tables(beads):
    modes = np.arange(beads)
    turn = 2.0 * STIFFNESS * np.sin(np.pi * modes / beads)
    safe = np.where(turn > 0, turn, 1.0)
    gain = np.where(turn > 0, np.sin(turn) / safe, 1.0)
    waves = np.cos(2.0 * np.pi * np.outer(modes, modes) / beads) / beads
    return waves @ np.cos(turn), waves @ gain, waves @ (turn * np.sin(turn))


def pick(table, index):
    return jnp.take_along_axis(table, index, axis=1, mode="promise_in_bounds")


def split_two(value):
    high = value.astype(BF16)
    return jnp.concatenate([high, (value - high.astype(F32)).astype(BF16)], axis=1)


def step_kernel(
    n_space, n_bead,
    pos_in, mom_in, mass_in, feat_in, near_in, image_in, face_in,
    query_in, key_in, value_in, probe_in, rate_in,
    new_pos, new_mom,
    pos, mom, mass, feat, near, image, w_query, w_key, w_value, w_probe, rate, load_sem,
    feat_halo, pos_halo, face_halo, peer_pos, peer_kick, kick,
    probes, dots_own, dots_halo, first, index_t, low_t, shift_t, own_t, offs, weights, scaled,
    feat_send, feat_recv, pos_send, pos_recv, face_send, face_recv,
    peer_send, peer_recv, kick_send, kick_recv,
):
    beads, atoms, channels = feat.shape
    near_count = near.shape[0]
    heads = rate.shape[0]
    head_size = channels // heads
    pairs = beads // 2
    terms = 2 * heads
    s = lax.axis_index("space")
    g = lax.axis_index("bead")
    upper = lax.rem(s + 1, n_space)
    lower = lax.rem(s + n_space - 1, n_space)
    peers = [lax.rem(g + r, n_bead) for r in range(1, n_bead)]

    def copy(src, dst, send, recv, target):
        return pltpu.make_async_remote_copy(
            src_ref=src, dst_ref=dst, send_sem=send, recv_sem=recv,
            device_id=target, device_id_type=pl.DeviceIdType.MESH,
        )

    barrier = pltpu.get_barrier_semaphore()
    for target in [(lower, g), (upper, g)] + [(s, q) for q in peers]:
        pl.semaphore_signal(barrier, inc=1, device_id=target, device_id_type=pl.DeviceIdType.MESH)

    loads = [
        pltpu.make_async_copy(src, dst, load_sem.at[i])
        for i, (src, dst) in enumerate(
            (
                (near_in, near), (image_in, image), (pos_in, pos),
                (feat_in, feat), (query_in, w_query), (probe_in, w_probe),
                (key_in, w_key), (value_in, w_value),
                (mom_in, mom), (mass_in, mass), (rate_in, rate),
            )
        )
    ]
    for c in loads:
        c.start()

    pl.semaphore_wait(barrier, 2 + len(peers))

    sides = [(0, (upper, g)), (1, (lower, g))]
    face_copies = [
        copy(face_in.at[1 - slot], face_halo.at[slot], face_send.at[slot], face_recv.at[slot], to)
        for slot, to in sides
    ]
    pos_copies = [
        copy(pos_in, pos_halo.at[slot], pos_send.at[slot], pos_recv.at[slot], to)
        for slot, to in sides
    ]
    feat_copies = [
        [
            copy(
                feat_in.at[b],
                feat_halo.at[b, pl.ds(slot * atoms, atoms)],
                feat_send.at[slot, b],
                feat_recv.at[slot, b],
                to,
            )
            for slot, to in sides
        ]
        for b in range(beads)
    ]
    peer_copies = [
        copy(
            pos_in, peer_pos.at[n_bead - r - 2], peer_send.at[r], peer_recv.at[n_bead - r - 2],
            (s, q),
        )
        for r, q in enumerate(peers)
    ]
    for c in face_copies + pos_copies:
        c.start()
    for both in feat_copies:
        for c in both:
            c.start()
    for c in peer_copies:
        c.start()

    for c in loads[:3]:
        c.wait()
    near2 = jnp.concatenate([near[...], near[...]], axis=0)
    index = jnp.transpose(near2)
    index_t[...] = index
    low_t[...] = jnp.bitwise_and(index, atoms - 1)
    code = image[...]
    one = lambda test: jnp.where(test, 1, 0)
    z = one(code >= 9) + one(code >= 18)
    rest = code - 9 * z
    y = one(rest >= 3) + one(rest >= 6)
    x = rest - 3 * y
    for c, part in enumerate((x, y, z)):
        shift = BOX_LENGTH * (part.astype(F32) - 1.0)
        shift_t[c] = jnp.transpose(jnp.concatenate([shift, shift], axis=0))
    for c in range(3):
        padded = jnp.concatenate([pos[c], jnp.zeros((8 - beads, atoms), F32)], axis=0)
        own_t[c] = jnp.transpose(padded)

    for c in loads[3:8]:
        c.wait()
    flat = feat[...].reshape(beads * atoms, channels)
    depth_head = lax.broadcasted_iota(jnp.int32, (channels, channels), 0) // head_size
    for kind, (into, out) in enumerate(((w_query, w_key), (w_probe, w_value))):
        small = split_two(jnp.dot(flat, into[...], preferred_element_type=F32))
        turned = jnp.transpose(out[...].astype(F32))
        wide = jnp.concatenate(
            [jnp.where(depth_head == h, turned, 0.0).astype(BF16) for h in range(heads)], axis=1
        )
        full = jnp.dot(small, jnp.concatenate([wide, wide], axis=0), preferred_element_type=F32)
        full = full.astype(BF16)
        for b in range(beads):
            for h in range(heads):
                probes[b, kind * heads + h] = full[
                    b * atoms : (b + 1) * atoms, h * channels : (h + 1) * channels
                ]

    half = lax.broadcasted_iota(jnp.int32, (ROWS, 2 * near_count), 1) < near_count
    chunks = atoms // ROWS
    share = terms // chunks

    def dot_share(b, table, into, i):
        some = pl.ds(i * share, share)
        width = table.shape[0]
        into[some] = lax.dot_general(
            probes[b, some].reshape(share * atoms, channels), table[...], NT,
            preferred_element_type=F32,
        ).reshape(share, atoms, width)

    def dot_all(b, table, into):
        into[...] = lax.dot_general(
            probes[b].reshape(terms * atoms, channels), table[...], NT, preferred_element_type=F32
        ).reshape(terms, atoms, table.shape[0])

    def pick_own(p, i):
        rows = pl.ds(pl.multiple_of(i * ROWS, ROWS), ROWS)
        low = low_t[rows, :]
        for e in range(terms):
            a = pick(dots_own[2 * p][e, rows, :], low)
            b = pick(dots_own[2 * p + 1][e, rows, :], low)
            first[p][e, rows, :] = jnp.where(half, a, b)

    def place(i):
        rows = pl.ds(pl.multiple_of(i * ROWS, ROWS), ROWS)
        low = low_t[rows, :]
        full = index_t[rows, :]
        is_own = full < atoms
        is_lower = full < 2 * atoms
        spread = lambda r: jnp.broadcast_to(r, (ROWS, atoms))
        from_lower = pick(spread(face_halo[0]), low)
        from_upper = pick(spread(face_halo[1]), low)
        low = jnp.where(is_own, low, jnp.where(is_lower, from_lower, from_upper))
        low_t[rows, :] = low
        for c in range(3):
            gaps = []
            for b in range(beads):
                line = [
                    pick(spread(r), low)
                    for r in (
                        pos[c, b : b + 1, :],
                        pos_halo[0, c, b : b + 1, :],
                        pos_halo[1, c, b : b + 1, :],
                    )
                ]
                found = jnp.where(is_own, line[0], jnp.where(is_lower, line[1], line[2]))
                gaps.append(
                    found - jnp.broadcast_to(own_t[c, rows, b : b + 1], (ROWS, 2 * near_count))
                )
            shift = shift_t[c, rows, :]
            for p in range(pairs):
                offs[p, c, rows, :] = jnp.where(half, gaps[2 * p], gaps[2 * p + 1]) + shift

    def halo_share(p, i):
        for b in (2 * p, 2 * p + 1):
            dot_share(b, feat_halo.at[b], dots_halo[b], i)

    for b in (0, 1):
        dot_all(b, feat.at[b], dots_own[b])

    for p in range(pairs - 1):

        def own_step(i, carry, p=p):
            pick_own(p, i)
            for b in (2 * p + 2, 2 * p + 3):
                dot_share(b, feat.at[b], dots_own[b], i)
            return carry

        lax.fori_loop(0, chunks, own_step, 0)

    for c in face_copies + pos_copies:
        c.wait_recv()

    def place_step(i, carry):
        place(i)
        return carry

    lax.fori_loop(0, chunks, place_step, 0)

    for b in (0, 1):
        for c in feat_copies[b]:
            c.wait_recv()

    def last_own_step(i, carry):
        pick_own(pairs - 1, i)
        halo_share(0, i)
        return carry

    lax.fori_loop(0, chunks, last_own_step, 0)

    for c in loads[8:]:
        c.wait()

    log2e = math.log2(math.e)
    sum_row = lax.broadcasted_iota(jnp.int32, (4 * near_count, 2 * near_count), 0)
    sum_col = lax.broadcasted_iota(jnp.int32, (4 * near_count, 2 * near_count), 1)
    same_half = (jnp.bitwise_and(sum_row, near_count) > 0) == (sum_col >= near_count)
    sum_table = jnp.where(same_half, 1.0, 0.0).astype(BF16)
    pick_row = lax.broadcasted_iota(jnp.int32, (8, 2 * near_count), 0)
    pick_col = lax.broadcasted_iota(jnp.int32, (8, 2 * near_count), 1)
    in_half = (pick_row == 0) == (pick_col < near_count)
    half_table = jnp.where(in_half & (pick_row < 2), 1.0, 0.0)
    kick_copies = []

    for p in range(pairs):
        if p + 1 < pairs:
            for b in (2 * p + 2, 2 * p + 3):
                for c in feat_copies[b]:
                    c.wait_recv()

        def attend(i, carry, p=p):
            rows = pl.ds(pl.multiple_of(i * ROWS, ROWS), ROWS)
            low = low_t[rows, :]
            full = index_t[rows, :]
            is_own = full < atoms
            is_lower = full < 2 * atoms
            off = [offs[p, c, rows, :] for c in range(3)]
            distance = off[0] * off[0] + off[1] * off[1] + off[2] * off[2]

            def term(e):
                found = []
                for b in (2 * p, 2 * p + 1):
                    a = pick(dots_halo[b][e, rows, 0:atoms], low)
                    c = pick(dots_halo[b][e, rows, atoms : 2 * atoms], low)
                    found.append(jnp.where(is_lower, a, c))
                return jnp.where(is_own, first[p][e, rows, :], jnp.where(half, found[0], found[1]))

            for h in range(heads):
                capped = jnp.tanh(term(h) * (1.0 / (SCORE_CAP * head_size**0.5)))
                weight = jnp.exp2(
                    capped * (SCORE_CAP * log2e) - distance * (rate[h] * log2e)
                )
                weights[h, rows, :] = weight
                scaled[h, rows, :] = weight * term(heads + h)
            if p + 1 < pairs:
                halo_share(p + 1, i)
            return carry

        lax.fori_loop(0, chunks, attend, 0)

        totals = jnp.dot(
            split_two(weights[...].reshape(heads * atoms, 2 * near_count)),
            sum_table,
            preferred_element_type=F32,
        ).reshape(heads, atoms, 2 * near_count)
        coupling = scaled[0] / totals[0]
        for h in range(1, heads):
            coupling = coupling + scaled[h] / totals[h]
        for c in range(3):
            force = lax.dot_general(
                half_table, coupling * offs[p, c], NT,
                precision=lax.Precision.HIGHEST, preferred_element_type=F32,
            ) * (1.0 / (heads * head_size**0.5))
            kick[p, c] = mom[c, 2 * p : 2 * p + 2, :] + force[0:2, :]
        for r, q in enumerate(peers):
            c = copy(
                kick.at[p],
                peer_kick.at[n_bead - r - 2, p],
                kick_send.at[r, p],
                kick_recv.at[n_bead - r - 2, p],
                (s, q),
            )
            c.start()
            kick_copies.append(c)

    total = beads * n_bead
    tables = step_tables(total)
    row = lax.broadcasted_iota(jnp.int32, (beads, atoms), 0)

    def column(table, source):
        result = jnp.full((beads, atoms), float(table[(0 - source) % total]), F32)
        for b in range(1, beads):
            result = jnp.where(row == b, float(table[(b - source) % total]), result)
        return result

    for c in peer_copies:
        c.wait_recv()
    kept_pos, moved, kept_mom, pulled = [[0.0] * 3 for _ in range(4)]
    for q in range(n_bead):
        if q == 1:
            for c in kick_copies:
                c.wait_recv()
        for j in range(beads):
            keep, gain, pull = [column(t, q * beads + j) for t in tables]
            for c in range(3):
                if q == 0:
                    where_pos = pos[c, j : j + 1, :]
                    where_kick = kick[j // 2, c, j % 2 : j % 2 + 1, :]
                else:
                    where_pos = peer_pos[q - 1, c, j : j + 1, :]
                    where_kick = peer_kick[q - 1, j // 2, c, j % 2 : j % 2 + 1, :]
                where_pos = jnp.broadcast_to(where_pos, (beads, atoms))
                where_kick = jnp.broadcast_to(where_kick, (beads, atoms))
                kept_pos[c] = kept_pos[c] + where_pos * keep
                moved[c] = moved[c] + where_kick * gain
                kept_mom[c] = kept_mom[c] + where_kick * keep
                pulled[c] = pulled[c] + where_pos * pull
    weight = mass[...]
    inverse = 1.0 / weight
    for c in range(3):
        new_pos[c] = kept_pos[c] + moved[c] * inverse
        new_mom[c] = kept_mom[c] - weight * pulled[c]

    for c in face_copies + pos_copies + peer_copies + kick_copies:
        c.wait_send()
    for both in feat_copies:
        for c in both:
            c.wait_send()


def hand_out(first_in, second_in, first_out, second_out, sems):
    copies = [
        pltpu.make_async_copy(first_in, first_out, sems.at[0]),
        pltpu.make_async_copy(second_in, second_out, sems.at[1]),
    ]
    for c in copies:
        c.start()
    for c in copies:
        c.wait()


def body(
    n_space, n_bead,
    positions, momenta, masses, features, neighbours, images, face_map,
    w_query, w_key, w_value, w_probe, radial_rate,
):
    beads, atoms, channels = features.shape
    heads = radial_rate.shape[0]
    near = neighbours.shape[0]
    terms = 2 * heads
    pairs = beads // 2
    wide = 2 * near
    peers = n_bead - 1
    vmem = pl.BlockSpec(memory_space=pltpu.VMEM)
    hbm = pl.BlockSpec(memory_space=pltpu.HBM)
    dma = pltpu.SemaphoreType.DMA
    shape = jax.ShapeDtypeStruct((3, beads, atoms), F32)
    square = pltpu.VMEM((channels, channels), BF16)
    new_positions, new_momenta = pl.pallas_call(
        functools.partial(step_kernel, n_space, n_bead),
        out_shape=(shape, shape),
        in_specs=[hbm] * 12,
        out_specs=(vmem, vmem),
        scratch_shapes=[
            pltpu.VMEM((3, beads, atoms), F32),
            pltpu.VMEM((3, beads, atoms), F32),
            pltpu.VMEM((1, atoms), F32),
            pltpu.VMEM((beads, atoms, channels), BF16),
            pltpu.VMEM((near, atoms), jnp.int32),
            pltpu.VMEM((near, atoms), jnp.int32),
            square, square, square, square,
            pltpu.SMEM((heads,), F32),
            dma((11,)),
            pltpu.VMEM((beads, 2 * atoms, channels), BF16),
            pltpu.VMEM((2, 3, beads, atoms), F32),
            pltpu.VMEM((2, 1, atoms), jnp.int32),
            pltpu.VMEM((peers, 3, beads, atoms), F32),
            pltpu.VMEM((peers, pairs, 3, 2, atoms), F32),
            pltpu.VMEM((pairs, 3, 2, atoms), F32),
            pltpu.VMEM((beads, terms, atoms, channels), BF16),
            tuple(pltpu.VMEM((terms, atoms, atoms), F32) for _ in range(beads)),
            tuple(pltpu.VMEM((terms, atoms, 2 * atoms), F32) for _ in range(beads)),
            tuple(pltpu.VMEM((terms, atoms, wide), F32) for _ in range(pairs)),
            pltpu.VMEM((atoms, wide), jnp.int32),
            pltpu.VMEM((atoms, wide), jnp.int32),
            pltpu.VMEM((3, atoms, wide), F32),
            pltpu.VMEM((3, atoms, 8), F32),
            pltpu.VMEM((pairs, 3, atoms, wide), F32),
            pltpu.VMEM((heads, atoms, wide), F32),
            pltpu.VMEM((heads, atoms, wide), F32),
            dma((2, beads)), dma((2, beads)), dma((2,)), dma((2,)), dma((2,)), dma((2,)),
            dma((peers,)), dma((peers,)), dma((peers, pairs)), dma((peers, pairs)),
        ],
        compiler_params=pltpu.CompilerParams(
            collective_id=0, has_side_effects=True, vmem_limit_bytes=VMEM_GRANT
        ),
    )(
        positions.transpose(1, 0, 2), momenta.transpose(1, 0, 2), masses.reshape(1, atoms),
        features, neighbours, images, face_map, w_query, w_key, w_value, w_probe, radial_rate,
    )
    new_positions, new_momenta = pl.pallas_call(
        hand_out,
        out_shape=(shape, shape),
        in_specs=[hbm] * 2,
        out_specs=(hbm, hbm),
        scratch_shapes=[dma((2,))],
        compiler_params=pltpu.CompilerParams(vmem_limit_bytes=VMEM_GRANT),
    )(new_positions, new_momenta)
    return new_positions.transpose(1, 0, 2), new_momenta.transpose(1, 0, 2)


def solution(mesh):
    placed = (
        P("bead", None, "space"),
        P("bead", None, "space"),
        P("space"),
        P("bead", "space", None),
        P(None, "space"),
        P(None, "space"),
        P(None, "space", None),
        P(),
        P(),
        P(),
        P(),
        P(),
    )
    return jax.shard_map(
        functools.partial(body, mesh.shape["space"], mesh.shape["bead"]),
        mesh=mesh,
        in_specs=placed,
        out_specs=(P("bead", None, "space"), P("bead", None, "space")),
        check_vma=False,
    )
```

time: 35 us -> 25 us (0.71); the launches traced: 34.4 us -> 24.9 us
  local copies, waits for them, and re-layouts: 8.01 us -> 0 us
  Pallas kernels: 25.7 us -> 24.2 us
    unnamed x24 -> x0, local copies, waits for them, and re-layouts: 6.82 us -> none
    pallas_call x1, Pallas kernels: 25.7 us -> 22.7 us  [body(): pl.pallas_call(functools.partial(step_kernel, n_space, n_bead), out_shape...]
    pallas_call x0 -> x1, Pallas kernels: none -> 1.49 us  [body(): pl.pallas_call(hand_out, out_shape=(shape, shape), in_specs=[hbm] * 2, ou...]
    pallas_call x2 -> x0, local copies, waits for them, and re-layouts: 1.19 us -> none  [body(): pl.pallas_call(functools.partial(step_kernel, n_space, n_bead), out_shape...]
where the time goes in v2:
time: 25 us; the launch traced here: 24.9 us
  Pallas kernels  24.2 us (97%)
  between operations  0.64 us (3%)
    pallas_call x1, Pallas kernels, body(): pl.pallas_call(functools.partial(step_kernel, n_space, n_bead), out_shape...  22.7 us
    pallas_call x1, Pallas kernels, body(): pl.pallas_call(hand_out, out_shape=(shape, shape), in_specs=[hbm] * 2, ou...  1.49 us

profile of v2, /device:TPU:0, one launch (start us, length us, event | category | flops | bytes accessed | tf_op | source)
XLA Modules:
  0.0 24.9 jit_solution(17402033392879141423)
XLA Ops:
  0.6 22.7 %shard_map.131 = (f32[3,4,128]{2,1,0:T(4,128)}, f32[3,4,128]{2,1,0:T(4,128)}) custom-call(f32[3,4,128]{2,1,0:T(4,128)} %bitcast.5, f32[3,4,128]{2,1,0:T(4,128)} %bitcast.6, f32[1,128]{1,0:T(1,128)} %bitcast.7, bf16[4,128,128]{2,1,0:T(8,128)(2,1)} %feat_in.1, s32[64,128]{1,0:T(8,128)} %near_in.1, s32[64,128]{1,0:T(8,128)} %image_in.1, s32[2,1,128]{2,1,0:T(1,128)} %face_in.1, ...), custom_call_target="tpu_custom_call" | custom-call | tf_op jit(solution)/shard_map/pallas_call | solution.py:403
  23.4 1.5 %shard_map.132 = (f32[3,4,128]{2,1,0:T(4,128)}, f32[3,4,128]{2,1,0:T(4,128)}) custom-call(f32[3,4,128]{2,1,0:T(4,128)} %get-tuple-element.6.first_in, f32[3,4,128]{2,1,0:T(4,128)} %get-tuple-element.7.second_in), custom_call_target="tpu_custom_call" | custom-call | tf_op jit(solution)/shard_map/pallas_call | solution.py:445

commit v3 on v2

--- a/solution.py
+++ b/solution.py
@@ -12,7 +12,7 @@
 STIFFNESS = 1.3
 BOX_LENGTH = 2.0
 SCORE_CAP = 30.0
-ROWS = 16
+ROWS = 32
 VMEM_GRANT = 64 * 2**20 - 2**14
 F32 = jnp.float32
 BF16 = jnp.bfloat16
@@ -234,19 +234,13 @@
 
     for c in face_copies + pos_copies:
         c.wait_recv()
-
-    def place_step(i, carry):
-        place(i)
-        return carry
-
-    lax.fori_loop(0, chunks, place_step, 0)
-
     for b in (0, 1):
         for c in feat_copies[b]:
             c.wait_recv()
 
     def last_own_step(i, carry):
         pick_own(pairs - 1, i)
+        place(i)
         halo_share(0, i)
         return carry
 
@@ -445,7 +439,7 @@
     new_positions, new_momenta = pl.pallas_call(
         hand_out,
         out_shape=(shape, shape),
-        in_specs=[hbm] * 2,
+        in_specs=[vmem] * 2,
         out_specs=(hbm, hbm),
         scratch_shapes=[dma((2,))],
         compiler_params=pltpu.CompilerParams(vmem_limit_bytes=VMEM_GRANT),

time: 25 us -> 27.2 us (1.088)
  Pallas kernels: 24.2 us -> 26.3 us
    pallas_call x1, Pallas kernels: 22.7 us -> 25 us  [body(): pl.pallas_call(functools.partial(step_kernel, n_space, n_bead), out_shape...]
where the time goes in v3:
time: 27.2 us; the launch traced here: 27 us
  Pallas kernels  26.3 us (97%)
  between operations  0.64 us (2%)
    pallas_call x1, Pallas kernels, body(): pl.pallas_call(functools.partial(step_kernel, n_space, n_bead), out_shape...  25 us
    pallas_call x1, Pallas kernels, body(): pl.pallas_call(hand_out, out_shape=(shape, shape), in_specs=[vmem] * 2, o...  1.32 us

profile of v3, /device:TPU:0, one launch (start us, length us, event | category | flops | bytes accessed | tf_op | source)
XLA Modules:
  0.0 27.0 jit_solution(4233867905551515803)
XLA Ops:
  0.6 25.0 %shard_map.131 = (f32[3,4,128]{2,1,0:T(4,128)}, f32[3,4,128]{2,1,0:T(4,128)}) custom-call(f32[3,4,128]{2,1,0:T(4,128)} %bitcast.5, f32[3,4,128]{2,1,0:T(4,128)} %bitcast.6, f32[1,128]{1,0:T(1,128)} %bitcast.7, bf16[4,128,128]{2,1,0:T(8,128)(2,1)} %feat_in.1, s32[64,128]{1,0:T(8,128)} %near_in.1, s32[64,128]{1,0:T(8,128)} %image_in.1, s32[2,1,128]{2,1,0:T(1,128)} %face_in.1, ...), custom_call_target="tpu_custom_call" | custom-call | tf_op jit(solution)/shard_map/pallas_call | solution.py:397
  25.7 1.3 %shard_map.132 = (f32[3,4,128]{2,1,0:T(4,128)}, f32[3,4,128]{2,1,0:T(4,128)}) custom-call(f32[3,4,128]{2,1,0:T(4,128)} %get-tuple-element.6.first_in, f32[3,4,128]{2,1,0:T(4,128)} %get-tuple-element.7.second_in), custom_call_target="tpu_custom_call" | custom-call | tf_op jit(solution)/shard_map/pallas_call | solution.py:439

commit v4 on v2

--- a/solution.py
+++ b/solution.py
@@ -12,7 +12,8 @@
 STIFFNESS = 1.3
 BOX_LENGTH = 2.0
 SCORE_CAP = 30.0
-ROWS = 16
+ROWS = 8
+BLOCKS = 2
 VMEM_GRANT = 64 * 2**20 - 2**14
 F32 = jnp.float32
 BF16 = jnp.bfloat16
@@ -161,7 +162,7 @@
                 ]
 
     half = lax.broadcasted_iota(jnp.int32, (ROWS, 2 * near_count), 1) < near_count
-    chunks = atoms // ROWS
+    chunks = atoms // (ROWS * BLOCKS)
     share = terms // chunks
 
     def dot_share(b, table, into, i):
@@ -225,9 +226,10 @@
     for p in range(pairs - 1):
 
         def own_step(i, carry, p=p):
-            pick_own(p, i)
             for b in (2 * p + 2, 2 * p + 3):
                 dot_share(b, feat.at[b], dots_own[b], i)
+            for k in range(BLOCKS):
+                pick_own(p, i * BLOCKS + k)
             return carry
 
         lax.fori_loop(0, chunks, own_step, 0)
@@ -236,7 +238,8 @@
         c.wait_recv()
 
     def place_step(i, carry):
-        place(i)
+        for k in range(BLOCKS):
+            place(i * BLOCKS + k)
         return carry
 
     lax.fori_loop(0, chunks, place_step, 0)
@@ -246,8 +249,9 @@
             c.wait_recv()
 
     def last_own_step(i, carry):
-        pick_own(pairs - 1, i)
         halo_share(0, i)
+        for k in range(BLOCKS):
+            pick_own(pairs - 1, i * BLOCKS + k)
         return carry
 
     lax.fori_loop(0, chunks, last_own_step, 0)
@@ -272,7 +276,7 @@
                 for c in feat_copies[b]:
                     c.wait_recv()
 
-        def attend(i, carry, p=p):
+        def attend(i, p=p):
             rows = pl.ds(pl.multiple_of(i * ROWS, ROWS), ROWS)
             low = low_t[rows, :]
             full = index_t[rows, :]
@@ -296,11 +300,15 @@
                 )
                 weights[h, rows, :] = weight
                 scaled[h, rows, :] = weight * term(heads + h)
+
+        def attend_step(i, carry, p=p, attend=attend):
             if p + 1 < pairs:
                 halo_share(p + 1, i)
+            for k in range(BLOCKS):
+                attend(i * BLOCKS + k)
             return carry
 
-        lax.fori_loop(0, chunks, attend, 0)
+        lax.fori_loop(0, chunks, attend_step, 0)
 
         totals = jnp.dot(
             split_two(weights[...].reshape(heads * atoms, 2 * near_count)),
@@ -445,7 +453,7 @@
     new_positions, new_momenta = pl.pallas_call(
         hand_out,
         out_shape=(shape, shape),
-        in_specs=[hbm] * 2,
+        in_specs=[vmem] * 2,
         out_specs=(hbm, hbm),
         scratch_shapes=[dma((2,))],
         compiler_params=pltpu.CompilerParams(vmem_limit_bytes=VMEM_GRANT),

time: 25 us -> 24.3 us (0.972)
  Pallas kernels: 24.2 us -> 23.5 us
    pallas_call x1, Pallas kernels: 22.7 us -> 22.2 us  [body(): pl.pallas_call(functools.partial(step_kernel, n_space, n_bead), out_shape...]
where the time goes in v4:
time: 24.3 us; the launch traced here: 24.1 us
  Pallas kernels  23.5 us (97%)
  between operations  0.64 us (3%)
    pallas_call x1, Pallas kernels, body(): pl.pallas_call(functools.partial(step_kernel, n_space, n_bead), out_shape...  22.2 us
    pallas_call x1, Pallas kernels, body(): pl.pallas_call(hand_out, out_shape=(shape, shape), in_specs=[vmem] * 2, o...  1.32 us

profile of v4, /device:TPU:0, one launch (start us, length us, event | category | flops | bytes accessed | tf_op | source)
XLA Modules:
  0.0 24.1 jit_solution(14322163223552437582)
XLA Ops:
  0.6 22.2 %shard_map.131 = (f32[3,4,128]{2,1,0:T(4,128)}, f32[3,4,128]{2,1,0:T(4,128)}) custom-call(f32[3,4,128]{2,1,0:T(4,128)} %bitcast.5, f32[3,4,128]{2,1,0:T(4,128)} %bitcast.6, f32[1,128]{1,0:T(1,128)} %bitcast.7, bf16[4,128,128]{2,1,0:T(8,128)(2,1)} %feat_in.1, s32[64,128]{1,0:T(8,128)} %near_in.1, s32[64,128]{1,0:T(8,128)} %image_in.1, s32[2,1,128]{2,1,0:T(1,128)} %face_in.1, ...), custom_call_target="tpu_custom_call" | custom-call | tf_op jit(solution)/shard_map/pallas_call | solution.py:411
  22.8 1.3 %shard_map.132 = (f32[3,4,128]{2,1,0:T(4,128)}, f32[3,4,128]{2,1,0:T(4,128)}) custom-call(f32[3,4,128]{2,1,0:T(4,128)} %get-tuple-element.6.first_in, f32[3,4,128]{2,1,0:T(4,128)} %get-tuple-element.7.second_in), custom_call_target="tpu_custom_call" | custom-call | tf_op jit(solution)/shard_map/pallas_call | solution.py:453
